TPU v7x, 256 devices: a whole 4x4x8 slice. The times are simulated.
256 devices in a mesh: tok: 32 (over z, y_lo, core), tp: 8 (over y_hi, x).
Axes of the slice: x: 4, y: 4 (y_hi: 2, y_lo: 2; y = y_hi * 2 + y_lo), z: 8, core: 2. Of those that a mesh axis runs over, the one named last changes fastest.
Arguments:
- hidden_in: bfloat16 [8192, 4096], P('tok', 'tp'), may hold values from -6 to 6
- norm_gain: float32 [4096], replicated, may hold values from 0.5 to 9, as said below
- w_query: bfloat16 [4096, 4096], P(None, 'tp'), may hold values from -0.09375 to 0.09375
- w_key: bfloat16 [4096, 1024], P(None, 'tp'), may hold values from -0.09375 to 0.09375
- w_value: bfloat16 [4096, 1024], P(None, 'tp'), may hold values from -0.09375 to 0.09375
- w_out: bfloat16 [4096, 4096], P('tp'), may hold values from -0.5 to 0.5
- doc_ids: int32 [8192], replicated, may hold values from 0 to 3, never falling along the last dimension, each value on 1 to 6144 neighbouring positions
Outputs:
- hidden_out: bfloat16 [8192, 4096], P('tok', 'tp')
- joint_cov: float32 [2, 4096, 2, 4096], P(None, 'tok', None, 'tp')
Inputs may be any that keep to these rules, and one draw needn't show every extreme that they name: `norm_gain`: each channel's gain is positive. `doc_ids`: document numbers never fall along the tokens; a document holds 1 to 6144 tokens.
All inputs are finite; a program needn't handle non-finite values.
Results may differ from a plain program's by a relative error of at most 0.013.
The roundings to bfloat16 on the way count: a program that leaves them out, or rounds other values in their place, can miss the bound.
Values may be sent and summed in bfloat16 or wider, within the bound.
No kernel may reach another device: no remote copies, remote signals or barrier semaphores. Data moves between devices by JAX's collectives and lax.ppermute only.
A program may use at most 128 MiB of HBM per device.

v0:
```python
import jax
import jax.numpy as jnp
from jax import lax
from jax.sharding import PartitionSpec as P

HS = 128
epsilon = 1e-05
rope_base = 500000.0


def laid_out(blocks, dim):
    blocks = jnp.moveaxis(blocks, 0, dim)
    dims = blocks.shape
    return blocks.reshape(*dims[:dim], dims[dim] * dims[dim + 1], *dims[dim + 2 :])


def copy_for_each(x, axis):
    copies = jnp.broadcast_to(x, (lax.axis_size(axis), *x.shape))
    return lax.all_to_all(copies, axis, split_axis=0, concat_axis=0, tiled=True)


def collect(x, axis, dim):
    return laid_out(copy_for_each(x, axis), dim)


def in_one_piece(arrays, axis, dim, along):
    ends, at = ([], 0)
    for a in arrays[:-1]:
        at += a.shape[along]
        ends.append(at)
    both = jnp.concatenate(arrays, axis=along)
    return tuple(jnp.split(lax.all_gather(both, axis, axis=dim, tiled=True), ends, axis=along))


def rotate(vectors, positions):
    half_dim = vectors.shape[-1] // 2
    inv_freq = rope_base ** (-(jnp.arange(half_dim, dtype=jnp.float32) * 2.0) / vectors.shape[-1])
    angles = positions.astype(jnp.float32)[:, None] * inv_freq[None, :]
    cosine = jnp.cos(angles)[:, None, :]
    sine_part = jnp.sin(angles)[:, None, :]
    first_half = vectors[..., :half_dim]
    second_half = vectors[..., half_dim:]
    return jnp.concatenate(
        [
            first_half * cosine - second_half * sine_part,
            second_half * cosine + first_half * sine_part,
        ],
        axis=-1,
    )


def on_device(hidden_in, norm_gain, w_query, w_key, w_value, w_out, doc_ids):
    tok_rows = hidden_in.shape[0]
    col_width = hidden_in.shape[1]
    tok_count = lax.axis_size("tok")
    tok_index = lax.axis_index("tok")
    tp_index = lax.axis_index("tp")
    all_rows = tok_rows * tok_count
    full_in = collect(hidden_in, "tp", 1)
    model_width = full_in.shape[1]
    row_width = model_width // tok_count
    widened = full_in.astype(jnp.float32)
    factor = lax.rsqrt(jnp.mean(widened * widened, axis=1, keepdims=True) + epsilon)
    normed = (widened * factor * norm_gain[None, :]).astype(jnp.bfloat16)
    kv_heads = w_key.shape[1] // HS
    groups = w_query.shape[1] // w_key.shape[1]
    first_row = tok_index * tok_rows
    positions = first_row + jnp.arange(tok_rows, dtype=jnp.int32)
    key_local = rotate(
        jnp.dot(normed, w_key, preferred_element_type=jnp.float32).reshape(tok_rows, kv_heads, HS),
        positions % all_rows,
    )
    key_local = key_local.astype(jnp.bfloat16).reshape(tok_rows, kv_heads * HS)
    value_local = jnp.dot(normed, w_value, preferred_element_type=jnp.float32).astype(jnp.bfloat16)
    key_rows, value_rows = in_one_piece((key_local, value_local), "tok", 0, 1)
    queries = rotate(
        jnp.dot(normed, w_query, preferred_element_type=jnp.float32).reshape(
            tok_rows, kv_heads * groups, HS
        ),
        positions % all_rows,
    )
    queries = queries.astype(jnp.bfloat16).reshape(tok_rows, kv_heads, groups, HS)
    key_seq = key_rows.reshape(all_rows, kv_heads, HS)
    value_seq = value_rows.reshape(all_rows, kv_heads, HS)
    key_pos = jnp.arange(all_rows, dtype=jnp.int32)
    query_doc = lax.dynamic_slice_in_dim(doc_ids, first_row, tok_rows, 0)
    allowed = (query_doc[:, None] == doc_ids[None, :]) & (key_pos[None, :] <= positions[:, None])
    scores = jnp.einsum(
        "qhgd,khd->hgqk", queries, key_seq, preferred_element_type=jnp.float32
    ) * HS ** (-0.5)
    scores = jnp.where(allowed[None, None], scores, -jnp.inf)
    row_max = jnp.max(scores, axis=-1, keepdims=True)
    weights = jnp.exp(scores - row_max)
    weight_sum = jnp.sum(weights, axis=-1, keepdims=True)
    blended = (
        jnp.einsum(
            "hgqk,khd->hgqd",
            weights.astype(jnp.bfloat16),
            value_seq,
            preferred_element_type=jnp.float32,
        )
        / weight_sum
    )
    attended = (
        jnp.transpose(blended, (2, 0, 1, 3))
        .astype(jnp.bfloat16)
        .reshape(tok_rows, kv_heads * groups * HS)
    )
    partial_out = jnp.dot(attended, w_out, preferred_element_type=jnp.float32)
    summed = lax.psum(partial_out, "tp")
    full_out = (widened + summed).astype(jnp.bfloat16)
    hidden_out = lax.dynamic_slice_in_dim(full_out, tp_index * col_width, col_width, 1)
    joint_local = jnp.stack(
        [
            full_in.reshape(tok_rows, tok_count, row_width),
            full_out.reshape(tok_rows, tok_count, row_width),
        ],
        axis=1,
    )
    row_block = lax.all_to_all(joint_local, "tok", split_axis=2, concat_axis=0, tiled=True).reshape(
        all_rows, 2 * row_width
    )
    portion = lax.all_gather(jnp.stack([hidden_in, hidden_out], axis=1), "tok", axis=0, tiled=True)
    piece_rows = portion.shape[0]
    flat_part = portion.reshape(piece_rows, 2 * col_width)
    product = lax.dot_general(
        row_block, flat_part, (((0,), (0,)), ((), ())), preferred_element_type=jnp.float32
    )
    col_sum = jnp.sum(flat_part, axis=0, dtype=jnp.float32)
    row_mean = jnp.sum(row_block, axis=0, dtype=jnp.float32) / all_rows
    col_mean = col_sum / all_rows
    joint_cov = (product / all_rows - row_mean[:, None] * col_mean[None, :]).reshape(
        2, row_width, 2, col_width
    )
    return (hidden_out, joint_cov)


def solution(mesh):
    return jax.shard_map(
        on_device,
        mesh=mesh,
        in_specs=(
            P("tok", "tp"),
            P(),
            P(None, "tp"),
            P(None, "tp"),
            P(None, "tp"),
            P("tp", None),
            P(),
        ),
        out_specs=(P("tok", "tp"), P(None, "tok", None, "tp")),
        check_vma=False,
    )
```

profile of v0, /device:TPU:1, one launch (start us, length us, event | category | flops | bytes accessed | tf_op | source)
XLA Modules:
  0.0 543.1 jit_solution(12067020020564749845)
XLA Ops:
  7.2 0.0 copy-start
  7.2 1.2 copy.29
  8.4 1.5 broadcast_in_dim.10
  9.8 7.5 %all-to-all-start = ((bf16[8,256,512]{1,2,0:T(8,128)(2,1)}), bf16[8,256,512]{1,2,0:T(8,128)(2,1)S(1)}, u32[]{:S(2)}, u32[]{:S(2)}) async-start(bf16[8,256,512]{1,2,0:T(8,128)(2,1)} %broadcast_in_dim.10), calls=%async_computation | async-start | bytes 4194304 | tf_op jit(solution)/shard_map/all_to_all | solution.py:19
  17.3 0.0 all-gather.3.cloned.1.call-start
  17.4 28.5 %all-to-all-done = bf16[8,256,512]{1,2,0:T(8,128)(2,1)S(1)} async-done(((bf16[8,256,512]{1,2,0:T(8,128)(2,1)}), bf16[8,256,512]{1,2,0:T(8,128)(2,1)S(1)}, u32[]{:S(2)}, u32[]{:S(2)}) %all-to-all-start) | async-done | bytes 2097184 | tf_op jit(solution)/shard_map/all_to_all | solution.py:19
  45.9 0.6 multiply_reduce_fusion
  46.5 2.3 bitcast_convert_fusion
  48.8 0.0 copy-start.7
  48.8 5.7 %copy.44 = f32[256,4096]{1,0:T(8,128)} copy(f32[256,4096]{0,1:T(8,128)} %bitcast.92) | data formatting | bytes 8388608 | tf_op jit(solution)/shard_map/convert_element_type | solution.py:62
  54.4 0.0 copy-done.7
  54.4 0.0 copy-start.5
  54.4 2.9 multiply_convert_fusion.1
  57.3 0.0 copy-done
  57.3 0.8 convolution_convert_fusion
  58.1 0.0 copy-done.5
  58.2 0.8 convolution_bitcast_fusion
  59.0 0.3 fusion.28
  59.3 0.7 pad_maximum_fusion.2
  60.0 0.0 all-gather.3.cloned.1.call-update
  60.0 0.2 all-reduce.2.cloned.1.call-start
  60.2 0.0 copy-start.8
  60.3 6.4 %copy.47 = bf16[512,4096]{1,0:T(8,128)(2,1)} copy(bf16[512,4096]{0,1:T(8,128)(2,1)} %bitcast.95) | data formatting | bytes 8388608 | tf_op jit(solution)/shard_map/dot_general | solution.py:77
  66.7 0.0 copy-done.8
  66.7 0.0 copy-start.4
  66.7 0.1 dynamic_slice.6
  66.8 0.3 multiply_cosine_fusion
  67.1 4.7 fusion.7
  71.8 0.7 multiply_convert_fusion
  72.5 0.0 copy-done.4
  72.5 1.3 fusion.34
  73.8 0.1 subtract_convert_fusion
  73.8 61.0 %all-gather.3.cloned.1.call-done = bf16[8192,256]{0,1:T(8,128)(2,1)} async-done(((bf16[256,256]{0,1:T(8,128)(2,1)}), bf16[8192,256]{0,1:T(8,128)(2,1)}) %all-gather.3.cloned.1.call-update) | async-done | bytes 4194320 | tf_op jit(solution)/shard_map/all_gather | solution.py:32
  134.9 0.0 copy-start.3
  134.9 15.3 %fusion.2 = (f32[4,256]{1,0:T(4,128)S(1)}, f32[8192,256,4]{1,0,2:T(8,128)}) fusion(pred[256,8192]{0,1:T(8,128)(4,1)} %fusion.7, bf16[256,4,64]{0,2,1:T(8,128)(2,1)S(1)} %get-tuple-element.3, bf16[256,4,64]{0,2,1:T(8,128)(2,1)S(1)} %get-tuple-element.2, bf16[8192,256]{0,1:T(8,128)(2,1)} %all-gather.3.cloned.1.call-done), kind=kOutput, calls=%fused_computation.5 | convolution fusion | flops 2173172736 | bytes 38014976 | tf_op jit(solution)/shard_map/qhgd,khd->hgqk/dot_general | solution.py:88
  150.2 0.0 copy-done.3
  150.2 14.5 %fusion = f32[4,256]{1,0:T(4,128)S(1)} fusion(f32[8192,256,4]{1,0,2:T(8,128)} %get-tuple-element.9, f32[4,256]{1,0:T(4,128)S(1)} %get-tuple-element.8, pred[256,8192]{0,1:T(8,128)(4,1)S(1)} %copy-done.3), kind=kLoop, calls=%fused_computation.3 | loop fusion | flops 33553408 | bytes 35659776 | tf_op jit(solution)/shard_map/reduce_sum | solution.py:94
  164.7 15.5 %fusion.13 = bf16[4,256,128]{1,2,0:T(8,128)(2,1)S(1)} fusion(f32[8192,256,4]{1,0,2:T(8,128)} %get-tuple-element.9, f32[4,256]{1,0:T(4,128)S(1)} %get-tuple-element.8, pred[256,8192]{0,1:T(8,128)(4,1)} %fusion.7, bf16[8192,256]{0,1:T(8,128)(2,1)} %all-gather.3.cloned.1.call-done, f32[4,256]{1,0:T(4,128)S(1)} %fusion), kind=kOutput, calls=%fused_computation.26 | convolution fusion | flops 2181300224 | bytes 38019072 | tf_op jit(solution)/shard_map/hgqk,khd->hgqd/dot_general | solution.py:96
  180.2 5.5 %fusion.35 = f32[256,4096]{1,0:T(8,128)} fusion(bf16[256,512]{0,1:T(8,128)(2,1)S(1)} %bitcast.100, bf16[512,4096]{1,0:T(8,128)(2,1)} %param.12), kind=kOutput, calls=%fused_computation.63 | convolution fusion | flops 1073741824 | bytes 8650752 | tf_op jit(solution)/shard_map/dot_general | solution.py:109
  185.6 0.0 all-reduce.2.cloned.1.call-update
  185.6 0.0 all-gather.5.cloned.1.call-start
  185.7 0.0 copy-start.6
  185.7 113.2 %all-reduce.2.cloned.1.call-done = f32[256,4096]{1,0:T(8,128)} async-done(((f32[256,4096]{1,0:T(8,128)}), f32[256,4096]{1,0:T(8,128)}) %all-reduce.2.cloned.1.call-update) | async-done | bytes 4194320 | tf_op jit(solution)/shard_map/psum | solution.py:110
  298.9 4.0 add_convert_fusion
  302.9 0.0 copy-start.2
  302.9 1.4 copy-done.2
  304.3 0.0 copy-done.6
  304.3 0.8 pad_maximum_fusion.1
  305.1 0.0 all-gather.5.cloned.1.call-update
  305.1 4.1 copy.48
  309.2 2.0 pad_maximum_fusion
  311.2 2.3 copy.37
  313.5 7.9 %all-to-all-start.1 = ((bf16[256,2,32,128]{0,3,1,2:T(8,128)(2,1)}), bf16[256,2,32,128]{0,3,1,2:T(8,128)(2,1)}, u32[]{:S(2)}, u32[]{:S(2)}) async-start(bf16[256,2,32,128]{0,3,1,2:T(8,128)(2,1)} %copy.37), calls=%async_computation.1 | async-start | bytes 8388608 | tf_op jit(solution)/shard_map/all_to_all | solution.py:120
  321.4 1.7 constant_dynamic-slice_fusion
  323.1 139.7 %all-to-all-done.1 = bf16[256,2,32,128]{0,3,1,2:T(8,128)(2,1)} async-done(((bf16[256,2,32,128]{0,3,1,2:T(8,128)(2,1)}), bf16[256,2,32,128]{0,3,1,2:T(8,128)(2,1)}, u32[]{:S(2)}, u32[]{:S(2)}) %all-to-all-start.1) | async-done | bytes 4194336 | tf_op jit(solution)/shard_map/all_to_all | solution.py:120
  462.8 4.6 copy.38
  467.4 6.4 %copy.49 = bf16[32,8,32,256]{3,1,2,0:T(8,128)(2,1)} copy(bf16[32,8,32,256]{3,2,1,0:T(8,128)(2,1)S(1)} %bitcast.93) | data formatting | bytes 8388608
  473.8 2.9 convert_reduce_fusion.1
  476.7 17.3 %all-gather.5.cloned.1.call-done = bf16[8192,2,512]{2,0,1:T(8,128)(2,1)} async-done(((bf16[256,2,512]{2,0,1:T(8,128)(2,1)}), bf16[8192,2,512]{2,0,1:T(8,128)(2,1)}) %all-gather.5.cloned.1.call-update) | async-done | bytes 16777232 | tf_op jit(solution)/shard_map/all_gather | solution.py:123
  494.0 10.3 %convert_reduce_fusion = f32[2,512]{1,0:T(2,128)S(1)} fusion(bf16[8192,2,512]{2,0,1:T(8,128)(2,1)} %all-gather.5.cloned.1.call-done), kind=kLoop, calls=%fused_computation.1 | loop fusion | flops 16776192 | bytes 16781312 | tf_op jit(solution)/shard_map/reduce_sum | solution.py:129
  504.4 20.9 %copy.39 = bf16[8192,2,512]{0,2,1:T(8,128)(2,1)} copy(bf16[8192,2,512]{2,0,1:T(8,128)(2,1)} %all-gather.5.cloned.1.call-done) | data formatting | bytes 33554432 | tf_op jit(solution)/shard_map/all_gather | solution.py:123
  525.3 9.4 %fusion.9 = f32[256,1024]{1,0:T(8,128)S(1)} fusion(bf16[8192,256]{0,1:T(8,128)(2,1)} %bitcast.97, bf16[8192,1024]{0,1:T(8,128)(2,1)} %bitcast.91, f32[1024]{0:T(1024)S(1)} %bitcast.101, f32[256]{0:T(256)S(1)} %multiply_bitcast_fusion.1), kind=kOutput, calls=%fused_computation.22 | convolution fusion | flops 4295753728 | bytes 22025216 | tf_op jit(solution)/shard_map/dot_general | solution.py:126
  534.7 1.9 reshape.283
  536.6 0.0 copy-done.1
  (10 shorter events, 0.1 us)
Async XLA Ops:
  7.2 50.1 %copy-start = (bf16[4096,128]{1,0:T(8,128)(2,1)S(1)}, bf16[4096,128]{1,0:T(8,128)(2,1)}, u32[]{:S(2)}) copy-start(bf16[4096,128]{1,0:T(8,128)(2,1)} %param.11) | copy-start | bytes 3145732
  9.8 36.0 %all-to-all-start = ((bf16[8,256,512]{1,2,0:T(8,128)(2,1)}), bf16[8,256,512]{1,2,0:T(8,128)(2,1)S(1)}, u32[]{:S(2)}, u32[]{:S(2)}) async-start(bf16[8,256,512]{1,2,0:T(8,128)(2,1)} %broadcast_in_dim.10), calls=%async_computation | async-start | bytes 4194304 | tf_op jit(solution)/shard_map/all_to_all | solution.py:19
  17.3 117.6 %all-gather.3.cloned.1.call-start = ((), (), s32[]{:S(2)}) async-start(), calls=%async_computation.2 | async-start | bytes 4325376 | tf_op jit(solution)/shard_map/all_gather | solution.py:32
  48.8 5.7 %copy-start.7 = (f32[4096]{0:T(1024)S(1)}, f32[4096]{0:T(1024)}, u32[]{:S(2)}) copy-start(f32[4096]{0:T(1024)} %param.8) | copy-start | bytes 49156
  54.4 3.7 copy-start.5
  60.0 238.9 %all-reduce.2.cloned.1.call-start = ((), (), s32[]{:S(2)}) async-start(), calls=%async_computation.3 | async-start | bytes 8388608 | tf_op jit(solution)/shard_map/psum | solution.py:110
  60.2 6.5 %copy-start.8 = (s32[8192]{0:T(1024)S(1)}, s32[8192]{0:T(1024)}, u32[]{:S(2)}) copy-start(s32[8192]{0:T(1024)} %param.13) | copy-start | bytes 98308
  66.7 5.8 %copy-start.4 = (bf16[512,4096]{1,0:T(8,128)(2,1)S(1)}, bf16[512,4096]{1,0:T(8,128)(2,1)}, u32[]{:S(2)}) copy-start(bf16[512,4096]{1,0:T(8,128)(2,1)} %copy.47) | copy-start | bytes 12582916
  134.9 15.3 %copy-start.3 = (pred[256,8192]{0,1:T(8,128)(4,1)S(1)}, pred[256,8192]{0,1:T(8,128)(4,1)}, u32[]{:S(2)}) copy-start(pred[256,8192]{0,1:T(8,128)(4,1)} %fusion.7) | copy-start | bytes 6291460
  185.6 308.4 %all-gather.5.cloned.1.call-start = ((), (), s32[]{:S(2)}) async-start(), calls=%async_computation.4 | async-start | bytes 17301504 | tf_op jit(solution)/shard_map/all_gather | solution.py:123
  185.7 118.6 %copy-start.6 = (bf16[256,512]{1,0:T(8,128)(2,1)S(1)}, bf16[256,512]{1,0:T(8,128)(2,1)}, u32[]{:S(2)}) copy-start(bf16[256,512]{1,0:T(8,128)(2,1)} %param.7) | copy-start | bytes 786436
  302.9 1.4 copy-start.2
  313.5 149.3 %all-to-all-start.1 = ((bf16[256,2,32,128]{0,3,1,2:T(8,128)(2,1)}), bf16[256,2,32,128]{0,3,1,2:T(8,128)(2,1)}, u32[]{:S(2)}, u32[]{:S(2)}) async-start(bf16[256,2,32,128]{0,3,1,2:T(8,128)(2,1)} %copy.37), calls=%async_computation.1 | async-start | bytes 8388608 | tf_op jit(solution)/shard_map/all_to_all | solution.py:120
  525.3 11.3 %copy-start.1 = (bf16[4096,128]{1,0:T(8,128)(2,1)S(1)}, bf16[4096,128]{1,0:T(8,128)(2,1)}, u32[]{:S(2)}) copy-start(bf16[4096,128]{1,0:T(8,128)(2,1)} %param.11) | copy-start | bytes 3145732
Sparse Core Ops, SparseCore 0:
  60.1 74.7 all-gather.2
  185.8 113.0 all-reduce.1
  305.3 188.7 all-gather.4
where the time goes:
time: 544 us; the launch traced here: 543 us
  waiting for transfers between devices  360 us (66%)
  local copies, waits for them, and re-layouts  58 us (11%)
  matrix products  48.6 us (9%)
  other arithmetic  47.1 us (9%)
  starting transfers between devices  15.7 us (3%)
  between operations  14 us (3%)
    all_to_all x1, waiting for transfers between devices, on_device(): lax.all_to_all(joint_local, 'tok', split_axis=2, concat_axis=0, tiled=True)  140 us
    psum x1, waiting for transfers between devices, on_device(): summed = lax.psum(partial_out, 'tp')  113 us
    all_gather x1, waiting for transfers between devices, in_one_piece(): lax.all_gather(both, axis, axis=dim, tiled=True)  61 us
    all_to_all x1, waiting for transfers between devices, copy_for_each(): return lax.all_to_all(copies, axis, split_axis=0, concat_axis=0, tiled=True)  28.5 us
    all_gather x1, local copies, waits for them, and re-layouts, on_device(): lax.all_gather(jnp.stack([hidden_in, hidden_out], axis=1), 'tok', axis=0,...  20.9 us
    all_gather x1, waiting for transfers between devices, on_device(): lax.all_gather(jnp.stack([hidden_in, hidden_out], axis=1), 'tok', axis=0,...  17.3 us
    dot_general x1, matrix products, on_device(): jnp.einsum('hgqk,khd->hgqd', weights.astype(jnp.bfloat16), value_seq, pre...  15.5 us
    dot_general x1, matrix products, on_device(): jnp.einsum('qhgd,khd->hgqk', queries, key_seq, preferred_element_type=jnp...  15.3 us
  transfers between devices with their start and end apart: 5, of which 5 were waited for; matrix products, arithmetic and copies ran while one was open for 7% of the time, Pallas kernels for 0%

commit v1 on v0

--- a/solution.py
+++ b/solution.py
@@ -120,7 +120,15 @@
     row_block = lax.all_to_all(joint_local, "tok", split_axis=2, concat_axis=0, tiled=True).reshape(
         all_rows, 2 * row_width
     )
-    portion = lax.all_gather(jnp.stack([hidden_in, hidden_out], axis=1), "tok", axis=0, tiled=True)
+    portion = jnp.concatenate(
+        lax.all_to_all(
+            jnp.stack([jnp.stack([hidden_in, hidden_out], axis=1)] * lax.axis_size("tok")),
+            "tok",
+            0,
+            0,
+        ),
+        axis=0,
+    )
     piece_rows = portion.shape[0]
     flat_part = portion.reshape(piece_rows, 2 * col_width)
     product = lax.dot_general(

time: 544 us -> 850 us (1.56)
  waiting for transfers between devices: 360 us -> 646 us
  local copies, waits for them, and re-layouts: 58 us -> 72 us
    all_to_all x0 -> x1, waiting for transfers between devices: none -> 351 us  [on_device(): lax.all_to_all(jnp.stack([jnp.stack([hidden_in, hidden_out], axis=1)] * l...]
    all_to_all x1, waiting for transfers between devices: 140 us -> 92.8 us  [on_device(): lax.all_to_all(joint_local, 'tok', split_axis=2, concat_axis=0, tiled=True)]
    all_gather x1 -> x0, local copies, waits for them, and re-layouts: 20.9 us -> none  [on_device(): lax.all_gather(jnp.stack([hidden_in, hidden_out], axis=1), 'tok', axis=0,...]
    all_gather x1 -> x0, waiting for transfers between devices: 17.3 us -> none  [on_device(): lax.all_gather(jnp.stack([hidden_in, hidden_out], axis=1), 'tok', axis=0,...]
    all_to_all x0 -> x1, local copies, waits for them, and re-layouts: none -> 15.5 us  [on_device(): lax.all_to_all(jnp.stack([jnp.stack([hidden_in, hidden_out], axis=1)] * l...]
    unnamed x21 -> x20, local copies, waits for them, and re-layouts: 8.93 us -> 21.3 us
  transfers between devices with their start and end apart: 5 -> 5, of which waited for: 5 -> 5; matrix products, arithmetic and copies ran while one was open for 7% -> 4% of each run, Pallas kernels for 0% -> 0%
where the time goes in v1:
time: 850 us; the launch traced here: 849 us
  waiting for transfers between devices  646 us (76%)
  local copies, waits for them, and re-layouts  72 us (8%)
  matrix products  48.8 us (6%)
  other arithmetic  44.1 us (5%)
  starting transfers between devices  23.5 us (3%)
  between operations  14.3 us (2%)
    all_to_all x1, waiting for transfers between devices, on_device(): lax.all_to_all(jnp.stack([jnp.stack([hidden_in, hidden_out], axis=1)] * l...  351 us
    psum x1, waiting for transfers between devices, on_device(): summed = lax.psum(partial_out, 'tp')  113 us
    all_to_all x1, waiting for transfers between devices, on_device(): lax.all_to_all(joint_local, 'tok', split_axis=2, concat_axis=0, tiled=True)  92.8 us
    all_gather x1, waiting for transfers between devices, in_one_piece(): lax.all_gather(both, axis, axis=dim, tiled=True)  61 us
    all_to_all x1, waiting for transfers between devices, copy_for_each(): return lax.all_to_all(copies, axis, split_axis=0, concat_axis=0, tiled=True)  28.5 us
    unnamed x20, local copies, waits for them, and re-layouts  21.3 us
  transfers between devices with their start and end apart: 5, of which 5 were waited for; matrix products, arithmetic and copies ran while one was open for 4% of the time, Pallas kernels for 0%

profile of v1, /device:TPU:1, one launch (start us, length us, event | category | flops | bytes accessed | tf_op | source)
XLA Modules:
  0.0 849.1 jit_solution(3518026693929016349)
XLA Ops:
  7.2 0.0 copy-start
  7.2 1.2 copy.63
  8.4 1.5 broadcast_in_dim.10
  9.8 7.5 all-to-all-start
  17.3 0.0 all-gather.2.cloned.1.call-start
  17.4 28.5 %all-to-all-done = bf16[8,256,512]{1,2,0:T(8,128)(2,1)S(1)} async-done(((bf16[8,256,512]{1,2,0:T(8,128)(2,1)}), bf16[8,256,512]{1,2,0:T(8,128)(2,1)S(1)}, u32[]{:S(2)}, u32[]{:S(2)}) %all-to-all-start) | async-done | bytes 2097184 | tf_op jit(solution)/shard_map/all_to_all | solution.py:19
  45.9 0.6 multiply_reduce_fusion
  46.5 2.3 bitcast_convert_fusion
  48.8 0.0 copy-start.6
  48.8 5.7 copy.80
  54.5 0.0 copy-done.6
  54.5 0.0 copy-start.4
  54.5 2.9 multiply_convert_fusion.1
  57.4 0.0 copy-done
  57.4 0.8 convolution_convert_fusion
  58.2 0.0 copy-done.4
  58.2 0.8 convolution_bitcast_fusion
  59.1 0.3 fusion.28
  59.4 0.7 pad_maximum_fusion.2
  60.1 0.0 all-gather.2.cloned.1.call-update
  60.1 0.2 all-reduce.2.cloned.1.call-start
  60.3 0.0 copy-start.7
  60.3 6.4 copy.83
  66.8 0.0 copy-done.7
  66.8 0.0 copy-start.3
  66.8 0.1 dynamic_slice.6
  66.9 0.3 multiply_cosine_fusion
  67.2 4.7 fusion.7
  71.9 0.7 multiply_convert_fusion
  72.6 0.0 copy-done.3
  72.6 1.3 fusion.34
  73.9 0.1 subtract_convert_fusion
  73.9 61.0 %all-gather.2.cloned.1.call-done = bf16[8192,256]{0,1:T(8,128)(2,1)} async-done(((bf16[256,256]{0,1:T(8,128)(2,1)}), bf16[8192,256]{0,1:T(8,128)(2,1)}) %all-gather.2.cloned.1.call-update) | async-done | bytes 4194320 | tf_op jit(solution)/shard_map/all_gather | solution.py:32
  135.0 15.3 %fusion.2 = (f32[4,256]{1,0:T(4,128)S(1)}, f32[8192,256,4]{1,0,2:T(8,128)}) fusion(pred[256,8192]{0,1:T(8,128)(4,1)} %fusion.7, bf16[256,4,64]{0,2,1:T(8,128)(2,1)S(1)} %get-tuple-element.3, bf16[256,4,64]{0,2,1:T(8,128)(2,1)S(1)} %get-tuple-element.2, bf16[8192,256]{0,1:T(8,128)(2,1)} %all-gather.2.cloned.1.call-done), kind=kOutput, calls=%fused_computation.5 | convolution fusion | flops 2173172736 | bytes 38014976 | tf_op jit(solution)/shard_map/qhgd,khd->hgqk/dot_general | solution.py:88
  150.3 0.0 copy-done.2
  150.3 14.5 %fusion = f32[4,256]{1,0:T(4,128)S(1)} fusion(f32[8192,256,4]{1,0,2:T(8,128)} %get-tuple-element.9, f32[4,256]{1,0:T(4,128)S(1)} %get-tuple-element.8, pred[256,8192]{0,1:T(8,128)(4,1)S(1)} %copy-done.2), kind=kLoop, calls=%fused_computation.3 | loop fusion | flops 33553408 | bytes 35659776 | tf_op jit(solution)/shard_map/reduce_sum | solution.py:94
  164.8 15.5 %fusion.13 = bf16[4,256,128]{1,2,0:T(8,128)(2,1)S(1)} fusion(f32[8192,256,4]{1,0,2:T(8,128)} %get-tuple-element.9, f32[4,256]{1,0:T(4,128)S(1)} %get-tuple-element.8, pred[256,8192]{0,1:T(8,128)(4,1)} %fusion.7, bf16[8192,256]{0,1:T(8,128)(2,1)} %all-gather.2.cloned.1.call-done, f32[4,256]{1,0:T(4,128)S(1)} %fusion), kind=kOutput, calls=%fused_computation.26 | convolution fusion | flops 2181300224 | bytes 38019072 | tf_op jit(solution)/shard_map/hgqk,khd->hgqd/dot_general | solution.py:96
  180.2 5.4 fusion.35
  185.7 0.0 all-reduce.2.cloned.1.call-update
  185.7 113.3 %all-reduce.2.cloned.1.call-done = f32[256,4096]{1,0:T(8,128)} async-done(((f32[256,4096]{1,0:T(8,128)}), f32[256,4096]{1,0:T(8,128)}) %all-reduce.2.cloned.1.call-update) | async-done | bytes 4194320 | tf_op jit(solution)/shard_map/psum | solution.py:110
  299.0 5.3 add_convert_fusion
  304.3 4.1 copy.84
  308.4 2.0 pad_maximum_fusion
  310.4 2.2 copy.71
  312.6 8.0 all-to-all-start.1
  320.6 1.0 fusion.46
  321.6 0.0 copy-done.5
  321.6 0.1 pad_maximum_fusion.1
  321.7 0.2 copy.73
  321.9 92.8 %all-to-all-done.1 = bf16[256,2,32,128]{0,3,1,2:T(8,128)(2,1)} async-done(((bf16[256,2,32,128]{0,3,1,2:T(8,128)(2,1)}), bf16[256,2,32,128]{0,3,1,2:T(8,128)(2,1)}, u32[]{:S(2)}, u32[]{:S(2)}) %all-to-all-start.1) | async-done | bytes 4194336 | tf_op jit(solution)/shard_map/all_to_all | solution.py:120
  414.7 5.9 stack.14
  420.6 7.7 all-to-all-start.2
  428.3 1.7 constant_dynamic-slice_fusion
  430.0 4.6 copy.72
  434.6 6.2 copy.86
  440.8 2.9 convert_reduce_fusion.1
  443.7 350.8 %all-to-all-done.2 = bf16[32,256,2,512]{1,3,2,0:T(8,128)(2,1)} async-done(((bf16[32,256,2,512]{1,3,2,0:T(8,128)(2,1)}), bf16[32,256,2,512]{1,3,2,0:T(8,128)(2,1)}, u32[]{:S(2)}, u32[]{:S(2)}) %all-to-all-start.2) | async-done | bytes 16777248 | tf_op jit(solution)/shard_map/all_to_all | solution.py:124
  794.5 15.5 %copy.74 = bf16[32,256,2,512]{1,0,3,2:T(8,128)(2,1)S(1)} copy(bf16[32,256,2,512]{1,3,2,0:T(8,128)(2,1)} %all-to-all-done.2) | data formatting | bytes 33554432 | tf_op jit(solution)/shard_map/all_to_all | solution.py:124
  810.0 13.8 %copy.87 = bf16[128,8,32,256]{3,1,2,0:T(8,128)(2,1)} copy(bf16[128,8,32,256]{3,2,1,0:T(8,128)(2,1)S(1)} %bitcast.94) | data formatting | bytes 33554432
  823.8 6.9 convert_reduce_fusion
  830.7 0.0 copy-start.1
  830.7 9.7 %fusion.9 = f32[256,1024]{1,0:T(8,128)S(1)} fusion(bf16[8192,256]{0,1:T(8,128)(2,1)} %bitcast.101, bf16[8192,1024]{0,1:T(8,128)(2,1)} %bitcast.96, f32[1024]{0:T(1024)S(1)} %bitcast.106, f32[256]{0:T(256)S(1)} %multiply_bitcast_fusion.1), kind=kOutput, calls=%fused_computation.22 | convolution fusion | flops 4295753728 | bytes 22025216 | tf_op jit(solution)/shard_map/dot_general | solution.py:134
  840.4 1.9 reshape.281
  842.3 0.0 copy-done.1
  (10 shorter events, 0.1 us)
Async XLA Ops:
  7.2 50.2 %copy-start = (bf16[4096,128]{1,0:T(8,128)(2,1)S(1)}, bf16[4096,128]{1,0:T(8,128)(2,1)}, u32[]{:S(2)}) copy-start(bf16[4096,128]{1,0:T(8,128)(2,1)} %param.11) | copy-start | bytes 3145732
  9.8 36.0 %all-to-all-start = ((bf16[8,256,512]{1,2,0:T(8,128)(2,1)}), bf16[8,256,512]{1,2,0:T(8,128)(2,1)S(1)}, u32[]{:S(2)}, u32[]{:S(2)}) async-start(bf16[8,256,512]{1,2,0:T(8,128)(2,1)} %broadcast_in_dim.10), calls=%async_computation | async-start | bytes 4194304 | tf_op jit(solution)/shard_map/all_to_all | solution.py:19
  17.3 117.6 %all-gather.2.cloned.1.call-start = ((), (), s32[]{:S(2)}) async-start(), calls=%async_computation.3 | async-start | bytes 4325376 | tf_op jit(solution)/shard_map/all_gather | solution.py:32
  48.8 5.7 copy-start.6
  54.5 3.7 copy-start.4
  60.1 238.9 %all-reduce.2.cloned.1.call-start = ((), (), s32[]{:S(2)}) async-start(), calls=%async_computation.4 | async-start | bytes 8388608 | tf_op jit(solution)/shard_map/psum | solution.py:110
  60.3 6.5 copy-start.7
  66.8 5.8 copy-start.3
  135.0 15.3 %copy-start.2 = (pred[256,8192]{0,1:T(8,128)(4,1)S(1)}, pred[256,8192]{0,1:T(8,128)(4,1)}, u32[]{:S(2)}) copy-start(pred[256,8192]{0,1:T(8,128)(4,1)} %fusion.7) | copy-start | bytes 6291460
  312.6 9.0 %copy-start.5 = (bf16[256,512]{1,0:T(8,128)(2,1)S(1)}, bf16[256,512]{1,0:T(8,128)(2,1)}, u32[]{:S(2)}) copy-start(bf16[256,512]{1,0:T(8,128)(2,1)} %param.7) | copy-start | bytes 786436
  312.6 102.1 %all-to-all-start.1 = ((bf16[256,2,32,128]{0,3,1,2:T(8,128)(2,1)}), bf16[256,2,32,128]{0,3,1,2:T(8,128)(2,1)}, u32[]{:S(2)}, u32[]{:S(2)}) async-start(bf16[256,2,32,128]{0,3,1,2:T(8,128)(2,1)} %copy.71), calls=%async_computation.1 | async-start | bytes 8388608 | tf_op jit(solution)/shard_map/all_to_all | solution.py:120
  420.6 373.9 %all-to-all-start.2 = ((bf16[32,256,2,512]{1,3,2,0:T(8,128)(2,1)}), bf16[32,256,2,512]{1,3,2,0:T(8,128)(2,1)}, u32[]{:S(2)}, u32[]{:S(2)}) async-start(bf16[32,256,2,512]{1,3,2,0:T(8,128)(2,1)} %stack.14), calls=%async_computation.2 | async-start | bytes 33554432 | tf_op jit(solution)/shard_map/all_to_all | solution.py:124
  830.7 11.5 %copy-start.1 = (bf16[4096,128]{1,0:T(8,128)(2,1)S(1)}, bf16[4096,128]{1,0:T(8,128)(2,1)}, u32[]{:S(2)}) copy-start(bf16[4096,128]{1,0:T(8,128)(2,1)} %param.11) | copy-start | bytes 3145732
Sparse Core Ops, SparseCore 0:
  60.2 74.7 all-gather.1
  185.8 113.1 all-reduce.1
